TPU v7x, 32 devices: a whole 2x2x4 slice. The times are simulated.
32 devices in a mesh: wide: 8 (over z, core), narrow: 4 (over y, x).
Axes of the slice: x: 2, y: 2, z: 4, core: 2. Of those that a mesh axis runs over, the one named last changes fastest.
Arguments:
- features: bfloat16 [4, 1024, 128], P('narrow', 'wide'), may hold values from -6 to 6
- weight: bfloat16 [128, 128], replicated, may hold values from -0.5 to 0.5
- tiles: bfloat16 [4, 1024, 8, 128], P('narrow', 'wide'), may hold values from -0.25 to 0.25
- tile_cols: int32 [4, 8, 8], P('narrow'), may hold values from 0 to 7, as said below
- tile_counts: int32 [4, 8], P('narrow'), may hold values from 2 to 8, as said below
- cotangent: bfloat16 [4, 1024, 128], P('narrow', 'wide'), may hold values from -6 to 6
Outputs:
- activated: bfloat16 [4, 1024, 128], P('narrow', 'wide')
- feature_grad: bfloat16 [4, 1024, 128], P('narrow', 'wide')
- weight_grad: float32 [128, 128], P('wide')
Inputs may be any that keep to these rules, and one draw needn't show every extreme that they name: `tile_cols`: slot 0 of each block row holds that block row's own diagonal tile (its column equals the block row); other slots may name any block column of the group, also repeatedly. `tile_counts`: each group has a block row that uses all 8 slots.
All inputs are finite; a program needn't handle non-finite values.
Results may differ from a plain program's by a relative error of at most 0.0062.
Values may be sent and summed in bfloat16 or wider, within the bound.
A program may use at most 64 MiB of HBM per device.

v0:
```python
import jax
import jax.numpy as jnp
from jax import lax
from jax.sharding import PartitionSpec as P


def shards(features, weight, tiles, tile_cols, tile_counts, cotangent):
    feat_local = features[0]
    row_count = feat_local.shape[0]
    feat_width = feat_local.shape[1]
    slot_count = tiles.shape[2]
    tile_size = tiles.shape[3]
    block_count = tile_cols.shape[1]
    local_blocks = max(row_count // tile_size, 1)
    rows_per = row_count // local_blocks
    first_block = lax.axis_index("wide") * row_count // tile_size
    cols_here = lax.dynamic_slice_in_dim(tile_cols[0], first_block, local_blocks, 0)
    counts_here = lax.dynamic_slice_in_dim(tile_counts[0], first_block, local_blocks, 0)
    alive_mask = jnp.arange(slot_count)[None, :] < counts_here[:, None]
    projected = jnp.dot(feat_local, weight, preferred_element_type=jnp.float32).astype(jnp.bfloat16)
    whole = lax.all_gather(projected, "wide", axis=0, tiled=True)
    stacked = whole.reshape(block_count, tile_size, feat_width)
    picked = stacked[cols_here] * alive_mask[:, :, None, None].astype(jnp.bfloat16)
    tile_local = tiles[0].reshape(local_blocks, rows_per, slot_count, tile_size)
    pre_act = jnp.einsum("bnst,bstd->bnd", tile_local, picked, preferred_element_type=jnp.float32)
    pre_act = pre_act.reshape(row_count, feat_width)
    sig_val = jax.nn.sigmoid(pre_act)
    activated = (pre_act * sig_val).astype(jnp.bfloat16)
    act_grad = (
        cotangent[0].astype(jnp.float32) * sig_val * (1.0 + pre_act * (1.0 - sig_val))
    ).astype(jnp.bfloat16)
    contrib = jnp.einsum(
        "bnst,bnd->bstd",
        tile_local,
        act_grad.reshape(local_blocks, rows_per, feat_width),
        preferred_element_type=jnp.float32,
    )
    seg_ids = jnp.where(alive_mask, cols_here, block_count).reshape(-1)
    summed = jax.ops.segment_sum(
        contrib.reshape(local_blocks * slot_count, tile_size, feat_width),
        seg_ids,
        num_segments=block_count + 1,
    )
    term = summed[:block_count].reshape(block_count * tile_size, feat_width)
    proj_grad = lax.psum_scatter(term, "wide", scatter_dimension=0, tiled=True).astype(jnp.bfloat16)
    feature_grad = lax.dot_general(
        proj_grad, weight, (((1,), (1,)), ((), ())), preferred_element_type=jnp.float32
    ).astype(jnp.bfloat16)
    weight_part = lax.dot_general(
        feat_local, proj_grad, (((0,), (0,)), ((), ())), preferred_element_type=jnp.float32
    )
    row_share = feat_width // lax.axis_size("wide")
    weight_total = lax.psum(weight_part, ("wide", "narrow"))
    weight_grad = lax.dynamic_slice_in_dim(
        weight_total, lax.axis_index("wide") * row_share, row_share, 0
    )
    return (activated[None], feature_grad[None], weight_grad)


def solution(mesh):
    placed = (
        P("narrow", "wide", None),
        P(),
        P("narrow", "wide", None, None),
        P("narrow", None, None),
        P("narrow", None),
        P("narrow", "wide", None),
    )
    return jax.shard_map(
        shards,
        mesh=mesh,
        in_specs=placed,
        out_specs=(P("narrow", "wide", None), P("narrow", "wide", None), P("wide", None)),
        check_vma=False,
    )
```

profile of v0, /device:TPU:0, one launch (start us, length us, event | category | flops | bytes accessed | tf_op | source)
XLA Modules:
  0.0 194.2 jit_solution(11305255537476850516)
XLA Ops:
  7.2 0.0 copy-start
  7.2 0.0 copy-start.4
  7.2 0.0 reduce-scatter.2.cloned.1.call-start
  7.3 0.6 copy-done.5
  7.9 0.6 constant_dynamic-slice_fusion.1
  8.5 0.7 fusion.15
  9.2 1.3 fusion.14
  10.5 0.6 compare_convert_fusion
  11.2 0.0 copy-start.2
  11.2 0.0 copy-start.3
  11.2 0.1 copy.17
  11.3 0.6 copy-done.2
  12.0 0.0 copy-done.3
  12.0 0.1 convolution_convert_fusion.1
  12.1 15.9 %all_gather.3 = bf16[1024,128]{1,0:T(8,128)(2,1)S(1)} all-gather(bf16[128,128]{1,0:T(8,128)(2,1)S(1)} %convolution_convert_fusion.1), channel_id=1, replica_groups=mesh['wide'=8,'narrow'=4] {'wide'}, dimensions={0}, use_global_device_ids=true | all-gather | bytes 294912 | tf_op jit(solution)/shard_map/all_gather | solution.py:21
  28.0 0.6 gather_fusion
  28.6 0.3 convolution_bitcast_fusion.2
  28.9 0.2 convolution_bitcast_fusion
  29.2 0.2 copy.19
  29.4 1.0 scatter_fusion
  30.5 0.8 slice.6
  31.3 0.0 reduce-scatter.2.cloned.1.call-update
  31.3 0.0 all-reduce.2.cloned.1.call-start
  31.4 0.7 copy.20
  32.1 31.4 %reduce-scatter.2.cloned.1.call-done = f32[128,128]{1,0:T(8,128)} async-done(((f32[1024,128]{1,0:T(8,128)}), f32[128,128]{1,0:T(8,128)}) %reduce-scatter.2.cloned.1.call-update) | async-done | bytes 65552 | tf_op jit(solution)/shard_map/reduce_scatter | solution.py:45
  63.5 1.6 convolution_bitcast_fusion.1
  65.2 0.0 all-reduce.2.cloned.1.call-update
  65.2 0.8 copy-done.1
  66.0 0.8 fusion
  66.8 119.0 %all-reduce.2.cloned.1.call-done = f32[128,128]{0,1:T(8,128)} async-done(((f32[128,128]{0,1:T(8,128)}), f32[128,128]{0,1:T(8,128)}) %all-reduce.2.cloned.1.call-update) | async-done | bytes 65552 | tf_op jit(solution)/shard_map/psum | solution.py:53
  185.8 0.9 constant_dynamic-slice_fusion
  186.7 0.7 copy.21
  (7 shorter events, 0.1 us)
Async XLA Ops:
  7.2 21.4 %copy-start = (bf16[1,128,8,128]{3,2,1,0:T(8,128)(2,1)S(1)}, bf16[1,128,8,128]{3,2,1,0:T(8,128)(2,1)}, u32[]{:S(2)}) copy-start(bf16[1,128,8,128]{3,2,1,0:T(8,128)(2,1)} %param.8) | copy-start | bytes 786436
  7.2 4.0 %copy-start.4 = (bf16[1,128,128]{2,1,0:T(8,128)(2,1)S(1)}, bf16[1,128,128]{2,1,0:T(8,128)(2,1)}, u32[]{:S(2)}) copy-start(bf16[1,128,128]{2,1,0:T(8,128)(2,1)} %param.11) | copy-start | bytes 98308
  7.2 56.3 %reduce-scatter.2.cloned.1.call-start = ((), (), s32[]{:S(2)}) async-start(), calls=%async_computation.1 | async-start | bytes 589824 | tf_op jit(solution)/shard_map/reduce_scatter | solution.py:45
  7.3 0.7 copy-start.5
  11.2 0.8 copy-start.2
  11.2 0.8 copy-start.3
  31.3 154.4 %all-reduce.2.cloned.1.call-start = ((), (), s32[]{:S(2)}) async-start(), calls=%async_computation.2 | async-start | bytes 131072 | tf_op jit(solution)/shard_map/psum | solution.py:53
  65.2 0.8 copy-start.1
Sparse Core Ops, SparseCore 0:
  31.4 32.0 reduce-scatter.1
  70.0 115.6 all-reduce.1
where the time goes:
time: 196 us; the launch traced here: 194 us
  waiting for transfers between devices  150 us (77%)
  blocking collectives  15.9 us (8%)
  between operations  14.2 us (7%)
  local copies, waits for them, and re-layouts  6.79 us (3%)
  other arithmetic  3.75 us (2%)
  matrix products  3.08 us (2%)
    psum x1, waiting for transfers between devices, shards(): weight_total = lax.psum(weight_part, ('wide', 'narrow'))  119 us
    reduce_scatter x1, waiting for transfers between devices, shards(): lax.psum_scatter(term, 'wide', scatter_dimension=0, tiled=True)  31.4 us
    all_gather x1, blocking collectives, shards(): whole = lax.all_gather(projected, 'wide', axis=0, tiled=True)  15.9 us
  transfers between devices with their start and end apart: 2, of which 2 were waited for; matrix products, arithmetic and copies ran while one was open for 1% of the time, Pallas kernels for 0%

commit v1 on v0

v1 whole, which is shorter than its diff:
```python
import functools

import jax
import jax.numpy as jnp
from jax import lax
from jax.experimental import pallas as pl
from jax.experimental.pallas import tpu as pltpu
from jax.sharding import PartitionSpec as P

MESH = pl.DeviceIdType.MESH
F32 = jnp.float32
BF16 = jnp.bfloat16


def selection(cols_ref, counts_ref, me, blocks, slots, chunk):
    shape = (blocks * chunk, chunk * slots)
    row = lax.broadcasted_iota(jnp.int32, shape, 0)
    lane = lax.broadcasted_iota(jnp.int32, (1, chunk * slots), 1)
    slot = lax.rem(lane, slots)
    node = lane // slots
    counts = counts_ref[...]
    here = lax.broadcasted_iota(jnp.int32, counts.shape, 1) == me
    count = jnp.sum(jnp.where(here, counts, 0), axis=1, keepdims=True)
    cols = cols_ref[0, pl.ds(me, 1), :]
    wanted = jnp.zeros((1, chunk * slots), jnp.int32)
    for s in range(slots):
        wanted = jnp.where(slot == s, cols[:, s:s + 1], wanted)
    wanted = jnp.where(slot < count, wanted * chunk + node, -1)
    return jnp.where(row == wanted, 1.0, 0.0).astype(BF16)


def kernel(
    wide, narrow, slots,
    cols_hbm, counts_hbm, feat_hbm, weight_hbm, tiles_hbm, cot_hbm,
    act_ref, fgrad_ref, wgrad_ref,
    cols_ref, counts_ref, weight_ref, tiles_ref, cot_ref, in_sems, gathered, adj, terms, incoming, wpart, wincoming, nbuf,
    f_send, f_recv, t_send, t_recv, w_send, w_recv, n_send, n_recv,
):
    me = lax.axis_index("wide")
    grp = lax.axis_index("narrow")
    nodes = feat_hbm.shape[1]
    tile = tiles_hbm.shape[1]
    chunk = tile // slots
    share = wgrad_ref.shape[0]

    def wide_peer(k):
        return lax.rem(me + k, wide)

    def narrow_peer(j):
        return lax.rem(grp + j, narrow)

    barrier = pltpu.get_barrier_semaphore()
    for k in range(1, wide):
        pl.semaphore_signal(barrier, inc=1, device_id={"wide": wide_peer(k)}, device_id_type=MESH)
    for j in range(1, narrow):
        pl.semaphore_signal(barrier, inc=1, device_id={"narrow": narrow_peer(j)}, device_id_type=MESH)

    def rows_of(index):
        return pl.ds(pl.multiple_of(index * tile, tile), tile)

    loads = [
        pltpu.make_async_copy(src, dst, in_sems.at[i])
        for i, (src, dst) in enumerate((
            (cols_hbm, cols_ref), (counts_hbm, counts_ref), (tiles_hbm, tiles_ref),
            (feat_hbm.at[0], gathered.at[rows_of(me)]), (weight_hbm, weight_ref), (cot_hbm, cot_ref)))
    ]
    for load in loads:
        load.start()
    pl.semaphore_wait(barrier, wide - 1 + narrow - 1)

    def feat_copy(slot, k):
        return pltpu.make_async_remote_copy(
            src_ref=feat_hbm.at[0], dst_ref=gathered.at[rows_of(slot)],
            send_sem=f_send.at[k - 1], recv_sem=f_recv.at[k - 1],
            device_id={"wide": wide_peer(k)}, device_id_type=MESH)

    for k in range(1, wide):
        feat_copy(me, k).start()
    for load in loads:
        load.wait()

    pick = selection(cols_ref, counts_ref, me, wide, slots, chunk)
    for j in range(nodes // chunk):
        part = jnp.dot(pick, tiles_ref[j * tile:(j + 1) * tile, :], preferred_element_type=F32).astype(BF16)
        for c in range(wide):
            adj[j * chunk:(j + 1) * chunk, c * tile:(c + 1) * tile] = part[c * chunk:(c + 1) * chunk]

    for k in range(1, wide):
        feat_copy(lax.rem(me - k + wide, wide), k).wait_recv()

    mixed = jnp.dot(adj[...], gathered[...], preferred_element_type=F32)
    mixed_hi = mixed.astype(BF16)
    mixed_lo = (mixed - mixed_hi.astype(F32)).astype(BF16)
    weight = weight_ref[...]
    pre_act = (jnp.dot(mixed_hi, weight, preferred_element_type=F32)
               + jnp.dot(mixed_lo, weight, preferred_element_type=F32))
    sig_val = jax.nn.sigmoid(pre_act)
    act_ref[0] = (pre_act * sig_val).astype(BF16)
    act_grad = (cot_ref[0].astype(F32) * sig_val * (1.0 + pre_act * (1.0 - sig_val))).astype(BF16)

    back = lax.dot_general(weight, act_grad, (((1,), (1,)), ((), ())), preferred_element_type=F32).astype(BF16)

    def term_copy(dest, k):
        return pltpu.make_async_remote_copy(
            src_ref=terms.at[dest], dst_ref=incoming.at[k - 1],
            send_sem=t_send.at[k - 1], recv_sem=t_recv.at[k - 1],
            device_id={"wide": wide_peer(k)}, device_id_type=MESH)

    for k in range(1, wide):
        dest = wide_peer(k)
        terms[dest] = jnp.dot(back, adj[:, rows_of(dest)], preferred_element_type=F32).astype(BF16)
        term_copy(dest, k).start()

    def weight_copy(dest, k):
        return pltpu.make_async_remote_copy(
            src_ref=wpart.at[dest], dst_ref=wincoming.at[k - 1],
            send_sem=w_send.at[k - 1], recv_sem=w_recv.at[k - 1],
            device_id={"wide": wide_peer(k)}, device_id_type=MESH)

    weight_part = lax.dot_general(
        mixed_hi, act_grad, (((0,), (0,)), ((), ())), preferred_element_type=F32)
    for c in range(wide):
        wpart[c] = weight_part[c * share:(c + 1) * share]
    for k in range(1, wide):
        weight_copy(wide_peer(k), k).start()

    own = jnp.dot(back, adj[:, rows_of(me)], preferred_element_type=F32)

    wsum = wpart[me]
    for k in range(1, wide):
        weight_copy(wide_peer(k), k).wait_recv()
        wsum = wsum + wincoming[k - 1]
    nbuf[grp] = wsum

    def narrow_copy(slot, j):
        return pltpu.make_async_remote_copy(
            src_ref=nbuf.at[slot], dst_ref=nbuf.at[slot],
            send_sem=n_send.at[j - 1], recv_sem=n_recv.at[j - 1],
            device_id={"narrow": narrow_peer(j)}, device_id_type=MESH)

    for j in range(1, narrow):
        narrow_copy(grp, j).start()

    for k in range(1, wide):
        term_copy(wide_peer(k), k).wait_recv()
        own = own + incoming[k - 1].astype(F32)
    fgrad_ref[0] = own.T.astype(BF16)

    for j in range(1, narrow):
        narrow_copy(lax.rem(grp - j + narrow, narrow), j).wait_recv()
    total = nbuf[0]
    for j in range(1, narrow):
        total = total + nbuf[j]
    wgrad_ref[...] = total

    for k in range(1, wide):
        feat_copy(me, k).wait_send()
        term_copy(wide_peer(k), k).wait_send()
        weight_copy(wide_peer(k), k).wait_send()
    for j in range(1, narrow):
        narrow_copy(grp, j).wait_send()


def shards(wide, narrow, features, weight, tiles, tile_cols, tile_counts, cotangent):
    _, nodes, width = features.shape
    slots, tile = tiles.shape[2:]
    if nodes != tile:
        raise ValueError("block rows")
    share = width // wide
    vmem = pl.BlockSpec(memory_space=pltpu.VMEM)
    hbm = pl.BlockSpec(memory_space=pltpu.HBM)
    dma = pltpu.SemaphoreType.DMA
    flops = 2 * nodes * tile * width * (2 * wide + wide + 4)
    return pl.pallas_call(
        functools.partial(kernel, wide, narrow, slots),
        out_shape=(
            jax.ShapeDtypeStruct((1, nodes, width), BF16),
            jax.ShapeDtypeStruct((1, nodes, width), BF16),
            jax.ShapeDtypeStruct((share, width), F32),
        ),
        in_specs=[hbm] * 6,
        out_specs=(vmem, vmem, vmem),
        scratch_shapes=[
            pltpu.VMEM(tile_cols.shape, jnp.int32),
            pltpu.VMEM(tile_counts.shape, jnp.int32),
            pltpu.VMEM(weight.shape, BF16),
            pltpu.VMEM((nodes * slots, tile), BF16),
            pltpu.VMEM(cotangent.shape, BF16),
            dma((6,)),
            pltpu.VMEM((wide * tile, width), BF16),
            pltpu.VMEM((nodes, wide * tile), BF16),
            pltpu.VMEM((wide, width, tile), BF16),
            pltpu.VMEM((wide - 1, width, tile), BF16),
            pltpu.VMEM((wide, share, width), F32),
            pltpu.VMEM((wide - 1, share, width), F32),
            pltpu.VMEM((narrow, share, width), F32),
            dma((wide - 1,)), dma((wide - 1,)),
            dma((wide - 1,)), dma((wide - 1,)),
            dma((wide - 1,)), dma((wide - 1,)),
            dma((narrow - 1,)), dma((narrow - 1,)),
        ],
        compiler_params=pltpu.CompilerParams(
            collective_id=0, has_side_effects=True, vmem_limit_bytes=32 * 1024 * 1024),
        cost_estimate=pl.CostEstimate(
            flops=flops, bytes_accessed=2 * nodes * width * (slots + 4), transcendentals=nodes * width),
        name="graph_layer",
    )(tile_cols, tile_counts, features, weight, tiles.reshape(nodes * slots, tile), cotangent)


def solution(mesh):
    placed = (
        P("narrow", "wide", None),
        P(),
        P("narrow", "wide", None, None),
        P("narrow", None, None),
        P("narrow", None),
        P("narrow", "wide", None),
    )
    return jax.shard_map(
        functools.partial(shards, mesh.shape["wide"], mesh.shape["narrow"]),
        mesh=mesh,
        in_specs=placed,
        out_specs=(P("narrow", "wide", None), P("narrow", "wide", None), P("wide", None)),
        check_vma=False,
    )
```

time: 196 us -> 32.8 us (0.17)
  waiting for transfers between devices: 150 us -> 0 us
  Pallas kernels: 0 us -> 25.4 us
  blocking collectives: 15.9 us -> 0 us
  between operations: 14.2 us -> 0.65 us
  other arithmetic: 3.75 us -> 0 us
  matrix products: 3.08 us -> 0 us
    psum x1 -> x0, waiting for transfers between devices: 119 us -> none  [shards(): weight_total = lax.psum(weight_part, ('wide', 'narrow'))]
    reduce_scatter x1 -> x0, waiting for transfers between devices: 31.4 us -> none  [shards(): lax.psum_scatter(term, 'wide', scatter_dimension=0, tiled=True)]
    pallas_call x0 -> x1, Pallas kernels: none -> 25.4 us  [shards(): pl.pallas_call(functools.partial(kernel, wide, narrow, slots), out_shape=...]
    all_gather x1 -> x0, blocking collectives: 15.9 us -> none  [shards(): whole = lax.all_gather(projected, 'wide', axis=0, tiled=True)]
    dot_general x5 -> x0, matrix products: 3.08 us -> none  [the longest x1 1.64 us: shards(): lax.dot_general(feat_local, proj_grad, (((0,), (0,)), ((), ())), preferre...]
    unnamed x15, local copies, waits for them, and re-layouts: 3.63 us -> 6.39 us
    select_n x2 -> x0, other arithmetic: 2.03 us -> none  [the longest x1 1.34 us: shards(): seg_ids = jnp.where(alive_mask, cols_here, block_count).reshape(-1)]
  transfers between devices with their start and end apart: 2 -> 0, of which waited for: 2 -> 0; matrix products, arithmetic and copies ran while one was open for 1% -> 0% of each run, Pallas kernels for 0% -> 0%
where the time goes in v1:
time: 32.8 us; the launch traced here: 32.4 us
  Pallas kernels  25.4 us (77%)
  local copies, waits for them, and re-layouts  6.39 us (19%)
  between operations  0.65 us (2%)
    pallas_call x1, Pallas kernels, shards(): pl.pallas_call(functools.partial(kernel, wide, narrow, slots), out_shape=...  25.4 us
    unnamed x15, local copies, waits for them, and re-layouts  6.39 us

profile of v1, /device:TPU:0, one launch (start us, length us, event | category | flops | bytes accessed | tf_op | source)
XLA Modules:
  0.0 32.4 jit_solution(9912580055361109580)
XLA Ops:
  0.6 0.0 copy-start.5
  0.6 0.6 %copy-done.5 = s32[1,8]{1,0:T(1,128)S(1)} copy-done((s32[1,8]{1,0:T(1,128)S(1)}, s32[1,8]{1,0:T(1,128)}, u32[]{:S(2)}) %copy-start.5) | copy-done | bytes 56
  1.3 0.0 copy-start
  1.3 0.9 %copy-done = bf16[1,128,8,128]{3,2,1,0:T(8,128)(2,1)S(1)} copy-done((bf16[1,128,8,128]{3,2,1,0:T(8,128)(2,1)S(1)}, bf16[1,128,8,128]{3,2,1,0:T(8,128)(2,1)}, u32[]{:S(2)}) %copy-start) | copy-done | bytes 262168
  2.2 0.0 copy-start.1
  2.2 0.8 %copy-done.1 = bf16[1,128,128]{2,1,0:T(8,128)(2,1)S(1)} copy-done((bf16[1,128,128]{2,1,0:T(8,128)(2,1)S(1)}, bf16[1,128,128]{2,1,0:T(8,128)(2,1)}, u32[]{:S(2)}) %copy-start.1) | copy-done | bytes 32792
  3.0 0.0 copy-start.2
  3.0 0.8 %copy-done.2 = bf16[128,128]{1,0:T(8,128)(2,1)S(1)} copy-done((bf16[128,128]{1,0:T(8,128)(2,1)S(1)}, bf16[128,128]{1,0:T(8,128)(2,1)}, u32[]{:S(2)}) %copy-start.2) | copy-done | bytes 32792
  3.8 0.0 copy-start.3
  3.8 0.8 %copy-done.3 = bf16[1,128,128]{2,1,0:T(8,128)(2,1)S(1)} copy-done((bf16[1,128,128]{2,1,0:T(8,128)(2,1)S(1)}, bf16[1,128,128]{2,1,0:T(8,128)(2,1)}, u32[]{:S(2)}) %copy-start.3) | copy-done | bytes 32792
  4.5 0.0 copy-start.4
  4.5 0.7 %copy-done.4 = s32[1,8,8]{2,1,0:T(8,128)S(1)} copy-done((s32[1,8,8]{2,1,0:T(8,128)S(1)}, s32[1,8,8]{2,1,0:T(8,128)}, u32[]{:S(2)}) %copy-start.4) | copy-done | bytes 280
  5.2 25.4 %graph_layer.1 = (bf16[1,128,128]{2,1,0:T(8,128)(2,1)S(1)}, bf16[1,128,128]{2,1,0:T(8,128)(2,1)S(1)}, f32[16,128]{1,0:T(8,128)S(1)}) custom-call(s32[1,8,8]{2,1,0:T(8,128)S(1)} %copy-done.4, s32[1,8]{1,0:T(1,128)S(1)} %copy-done.5, bf16[1,128,128]{2,1,0:T(8,128)(2,1)S(1)} %copy-done.1, bf16[128,128]{1,0:T(8,128)(2,1)S(1)} %copy-done.2, ...), custom_call_target="tpu_custom_call" | custom-call | flops 117440512 | bytes 393216 | tf_op jit(solution)/shard_map/graph_layer/pallas_call | solution.py:174
  30.6 0.6 %copy.12 = bf16[1,128,128]{2,1,0:T(8,128)(2,1)} copy(bf16[1,128,128]{2,1,0:T(8,128)(2,1)S(1)} %get-tuple-element.6) | data formatting | bytes 65536
  31.2 0.6 %copy.13 = bf16[1,128,128]{2,1,0:T(8,128)(2,1)} copy(bf16[1,128,128]{2,1,0:T(8,128)(2,1)S(1)} %get-tuple-element.7) | data formatting | bytes 65536
  31.8 0.6 %copy.14 = f32[16,128]{1,0:T(8,128)} copy(f32[16,128]{1,0:T(8,128)S(1)} %get-tuple-element.8) | data formatting | bytes 16384
Async XLA Ops:
  0.6 0.7 %copy-start.5 = (s32[1,8]{1,0:T(1,128)S(1)}, s32[1,8]{1,0:T(1,128)}, u32[]{:S(2)}) copy-start(s32[1,8]{1,0:T(1,128)} %counts_hbm.1) | copy-start | bytes 100
  1.3 0.9 %copy-start = (bf16[1,128,8,128]{3,2,1,0:T(8,128)(2,1)S(1)}, bf16[1,128,8,128]{3,2,1,0:T(8,128)(2,1)}, u32[]{:S(2)}) copy-start(bf16[1,128,8,128]{3,2,1,0:T(8,128)(2,1)} %param.8) | copy-start | bytes 786436
  2.2 0.8 %copy-start.1 = (bf16[1,128,128]{2,1,0:T(8,128)(2,1)S(1)}, bf16[1,128,128]{2,1,0:T(8,128)(2,1)}, u32[]{:S(2)}) copy-start(bf16[1,128,128]{2,1,0:T(8,128)(2,1)} %feat_hbm.1) | copy-start | bytes 98308
  3.0 0.8 %copy-start.2 = (bf16[128,128]{1,0:T(8,128)(2,1)S(1)}, bf16[128,128]{1,0:T(8,128)(2,1)}, u32[]{:S(2)}) copy-start(bf16[128,128]{1,0:T(8,128)(2,1)} %weight_hbm.1) | copy-start | bytes 98308
  3.8 0.8 %copy-start.3 = (bf16[1,128,128]{2,1,0:T(8,128)(2,1)S(1)}, bf16[1,128,128]{2,1,0:T(8,128)(2,1)}, u32[]{:S(2)}) copy-start(bf16[1,128,128]{2,1,0:T(8,128)(2,1)} %cot_hbm.1) | copy-start | bytes 98308
  4.5 0.7 %copy-start.4 = (s32[1,8,8]{2,1,0:T(8,128)S(1)}, s32[1,8,8]{2,1,0:T(8,128)}, u32[]{:S(2)}) copy-start(s32[1,8,8]{2,1,0:T(8,128)} %cols_hbm.1) | copy-start | bytes 772

commit v2 on v1

v2 whole, which is shorter than its diff:
```python
import functools

import jax
import jax.numpy as jnp
from jax import lax
from jax.experimental import pallas as pl
from jax.experimental.pallas import tpu as pltpu
from jax.sharding import PartitionSpec as P

MESH = pl.DeviceIdType.MESH
F32 = jnp.float32
BF16 = jnp.bfloat16
VMEM_LIMIT = 60 * 1024 * 1024


def selection(cols_ref, counts_ref, row_block, blocks, slots, chunk):
    shape = (blocks * chunk, chunk * slots)
    row = lax.broadcasted_iota(jnp.int32, shape, 0)
    lane = lax.broadcasted_iota(jnp.int32, (1, chunk * slots), 1)
    slot = lax.rem(lane, slots)
    node = lane // slots
    counts = counts_ref[...]
    here = lax.broadcasted_iota(jnp.int32, counts.shape, 1) == row_block
    count = jnp.sum(jnp.where(here, counts, 0), axis=1, keepdims=True)
    cols = cols_ref[0, pl.ds(row_block, 1), :]
    wanted = jnp.zeros((1, chunk * slots), jnp.int32)
    for s in range(slots):
        wanted = jnp.where(slot == s, cols[:, s:s + 1], wanted)
    wanted = jnp.where(slot < count, wanted * chunk + node, -1)
    return jnp.where(row == wanted, 1.0, 0.0).astype(BF16)


def partner(z, k):
    bit, out = 1, z
    while bit <= k:
        if k & bit:
            out = out + bit - 2 * bit * lax.rem(z // bit, 2)
        bit *= 2
    return out


def partner_order(count):
    order, half = [], count // 2
    while half:
        order += list(range(half, 2 * half))
        half //= 2
    return order


def kernel(
    wide, narrow, slots,
    cols_hbm, counts_hbm, feat_hbm, weight_hbm, tiles_hbm, cot_hbm,
    act_ref, fgrad_ref, wgrad_ref,
    cols_ref, counts_ref, weight_ref, tiles_ref, cot_ref, gathered, adj, acts, terms, incoming, wpart, wincoming, nbuf,
    in_sems, f_send, f_recv, x_send, x_recv, s_send, s_recv, t_send, t_recv, w_send, w_recv, n_send, n_recv,
):
    me = lax.axis_index("wide")
    grp = lax.axis_index("narrow")
    zs = wide // 2
    z, core = me // 2, lax.rem(me, 2)
    other = 1 - core
    sibling = 2 * z + other
    nodes = feat_hbm.shape[1]
    tile = tiles_hbm.shape[1]
    chunk = tile // slots
    share = wgrad_ref.shape[0]
    order = partner_order(zs)

    def peer(k):
        return 2 * partner(z, k) + core

    def narrow_peer(j):
        return lax.rem(grp + j, narrow)

    barrier = pltpu.get_barrier_semaphore()
    for k in order:
        pl.semaphore_signal(barrier, inc=1, device_id={"wide": peer(k)}, device_id_type=MESH)
    pl.semaphore_signal(barrier, inc=1, device_id={"wide": sibling}, device_id_type=MESH)
    for j in range(1, narrow):
        pl.semaphore_signal(barrier, inc=1, device_id={"narrow": narrow_peer(j)}, device_id_type=MESH)

    def rows_of(index):
        return pl.ds(pl.multiple_of(index * tile, tile), tile)

    loads = [
        pltpu.make_async_copy(src, dst, in_sems.at[i])
        for i, (src, dst) in enumerate((
            (cols_hbm, cols_ref), (counts_hbm, counts_ref), (tiles_hbm, tiles_ref.at[core]),
            (feat_hbm.at[0], gathered.at[rows_of(me)]), (weight_hbm, weight_ref),
            (cot_hbm.at[0], cot_ref.at[core])))
    ]
    for load in loads:
        load.start()
    pl.semaphore_wait(barrier, zs + narrow - 1)

    def feat_copy(k, slot):
        return pltpu.make_async_remote_copy(
            src_ref=feat_hbm.at[0], dst_ref=gathered.at[rows_of(slot)],
            send_sem=f_send.at[k - 1], recv_sem=f_recv.at[k - 1],
            device_id={"wide": peer(k)}, device_id_type=MESH)

    def forward_copy(k, slot):
        return pltpu.make_async_remote_copy(
            src_ref=gathered.at[rows_of(slot)], dst_ref=gathered.at[rows_of(slot)],
            send_sem=x_send.at[k - 1], recv_sem=x_recv.at[k - 1],
            device_id={"wide": sibling}, device_id_type=MESH)

    def swap_copies(half, slot):
        pairs = ((tiles_hbm, tiles_ref.at[half]), (feat_hbm.at[0], gathered.at[rows_of(slot)]),
                 (cot_hbm.at[0], cot_ref.at[half]))
        return [
            pltpu.make_async_remote_copy(
                src_ref=src, dst_ref=dst, send_sem=s_send.at[i], recv_sem=s_recv.at[i],
                device_id={"wide": sibling}, device_id_type=MESH)
            for i, (src, dst) in enumerate(pairs)
        ]

    for k in order:
        feat_copy(k, me).start()
    for copy in swap_copies(core, me):
        copy.start()
    for load in loads:
        load.wait()

    def build(half):
        pick = selection(cols_ref, counts_ref, 2 * z + half, wide, slots, chunk)
        base = half * nodes
        for j in range(nodes // chunk):
            part = jnp.dot(
                pick, tiles_ref[half, j * tile:(j + 1) * tile, :], preferred_element_type=F32).astype(BF16)
            rows = pl.ds(pl.multiple_of(base + j * chunk, chunk), chunk)
            for c in range(wide):
                adj[rows, c * tile:(c + 1) * tile] = part[c * chunk:(c + 1) * chunk]

    build(core)
    swapped = swap_copies(other, sibling)
    swapped[0].wait_recv()
    build(other)
    for k in order:
        feat_copy(k, peer(k)).wait_recv()
        forward_copy(k, peer(k)).start()
    swapped[1].wait_recv()
    swapped[2].wait_recv()
    for k in order:
        forward_copy(k, 2 * partner(z, k) + other).wait_recv()

    mixed = jnp.dot(adj[...], gathered[...], preferred_element_type=F32)
    mixed_hi = mixed.astype(BF16)
    mixed_lo = (mixed - mixed_hi.astype(F32)).astype(BF16)
    weight = weight_ref[...]
    pre_act = (jnp.dot(mixed_hi, weight, preferred_element_type=F32)
               + jnp.dot(mixed_lo, weight, preferred_element_type=F32))
    sig_val = jax.nn.sigmoid(pre_act)
    acts[...] = (pre_act * sig_val).astype(BF16).reshape(acts.shape)
    cot = cot_ref[...].reshape(2 * nodes, -1).astype(F32)
    act_grad = (cot * sig_val * (1.0 + pre_act * (1.0 - sig_val))).astype(BF16)

    def weight_copy(k):
        return pltpu.make_async_remote_copy(
            src_ref=wpart.at[peer(k)], dst_ref=wincoming.at[k - 1],
            send_sem=w_send.at[k - 1], recv_sem=w_recv.at[k - 1],
            device_id={"wide": peer(k)}, device_id_type=MESH)

    weight_part = lax.dot_general(
        mixed_hi, act_grad, (((0,), (0,)), ((), ())), preferred_element_type=F32)
    for c in range(wide):
        wpart[c] = weight_part[c * share:(c + 1) * share]
    for k in order:
        weight_copy(k).start()

    back = lax.dot_general(weight, act_grad, (((1,), (1,)), ((), ())), preferred_element_type=F32).astype(BF16)

    def term_copy(k):
        return pltpu.make_async_remote_copy(
            src_ref=terms.at[k - 1], dst_ref=incoming.at[k - 1],
            send_sem=t_send.at[k - 1], recv_sem=t_recv.at[k - 1],
            device_id={"wide": peer(k)}, device_id_type=MESH)

    for k in order:
        terms[k - 1] = jnp.dot(back, adj[:, rows_of(peer(k))], preferred_element_type=F32).astype(BF16)
        term_copy(k).start()

    own = jnp.dot(back, adj[:, rows_of(me)], preferred_element_type=F32)
    act_ref[0] = acts[core]

    wsum = wpart[me]
    for k in order:
        weight_copy(k).wait_recv()
        wsum = wsum + wincoming[k - 1]
    nbuf[grp] = wsum

    def narrow_copy(j, slot):
        return pltpu.make_async_remote_copy(
            src_ref=nbuf.at[slot], dst_ref=nbuf.at[slot],
            send_sem=n_send.at[j - 1], recv_sem=n_recv.at[j - 1],
            device_id={"narrow": narrow_peer(j)}, device_id_type=MESH)

    for j in range(1, narrow):
        narrow_copy(j, grp).start()

    for k in order:
        term_copy(k).wait_recv()
        own = own + incoming[k - 1].astype(F32)
    fgrad_ref[0] = own.T.astype(BF16)

    for j in range(1, narrow):
        narrow_copy(j, lax.rem(grp - j + narrow, narrow)).wait_recv()
    total = nbuf[0]
    for j in range(1, narrow):
        total = total + nbuf[j]
    wgrad_ref[...] = total

    for copy in swap_copies(core, me):
        copy.wait_send()
    for k in order:
        feat_copy(k, me).wait_send()
        forward_copy(k, peer(k)).wait_send()
        weight_copy(k).wait_send()
        term_copy(k).wait_send()
    for j in range(1, narrow):
        narrow_copy(j, grp).wait_send()


def shards(wide, narrow, features, weight, tiles, tile_cols, tile_counts, cotangent):
    _, nodes, width = features.shape
    slots, tile = tiles.shape[2:]
    zs = wide // 2
    if nodes != tile or 2 * zs != wide or zs & (zs - 1):
        raise ValueError("mesh shape")
    share = width // wide
    vmem = pl.BlockSpec(memory_space=pltpu.VMEM)
    hbm = pl.BlockSpec(memory_space=pltpu.HBM)
    dma = pltpu.SemaphoreType.DMA
    flops = 2 * nodes * tile * width * (5 * wide + 8)
    return pl.pallas_call(
        functools.partial(kernel, wide, narrow, slots),
        out_shape=(
            jax.ShapeDtypeStruct((1, nodes, width), BF16),
            jax.ShapeDtypeStruct((1, nodes, width), BF16),
            jax.ShapeDtypeStruct((share, width), F32),
        ),
        in_specs=[hbm] * 6,
        out_specs=(vmem, vmem, vmem),
        scratch_shapes=[
            pltpu.VMEM(tile_cols.shape, jnp.int32),
            pltpu.VMEM(tile_counts.shape, jnp.int32),
            pltpu.VMEM(weight.shape, BF16),
            pltpu.VMEM((2, nodes * slots, tile), BF16),
            pltpu.VMEM((2, nodes, width), BF16),
            pltpu.VMEM((wide * tile, width), BF16),
            pltpu.VMEM((2 * nodes, wide * tile), BF16),
            pltpu.VMEM((2, nodes, width), BF16),
            pltpu.VMEM((zs - 1, width, tile), BF16),
            pltpu.VMEM((zs - 1, width, tile), BF16),
            pltpu.VMEM((wide, share, width), F32),
            pltpu.VMEM((zs - 1, share, width), F32),
            pltpu.VMEM((narrow, share, width), F32),
            dma((6,)),
            dma((zs - 1,)), dma((zs - 1,)),
            dma((zs - 1,)), dma((zs - 1,)),
            dma((3,)), dma((3,)),
            dma((zs - 1,)), dma((zs - 1,)),
            dma((zs - 1,)), dma((zs - 1,)),
            dma((narrow - 1,)), dma((narrow - 1,)),
        ],
        compiler_params=pltpu.CompilerParams(
            collective_id=0, has_side_effects=True, vmem_limit_bytes=VMEM_LIMIT),
        cost_estimate=pl.CostEstimate(
            flops=flops, bytes_accessed=2 * nodes * width * (slots + 4), transcendentals=2 * nodes * width),
        name="graph_layer",
    )(tile_cols, tile_counts, features, weight, tiles.reshape(nodes * slots, tile), cotangent)


def solution(mesh):
    placed = (
        P("narrow", "wide", None),
        P(),
        P("narrow", "wide", None, None),
        P("narrow", None, None),
        P("narrow", None),
        P("narrow", "wide", None),
    )
    return jax.shard_map(
        functools.partial(shards, mesh.shape["wide"], mesh.shape["narrow"]),
        mesh=mesh,
        in_specs=placed,
        out_specs=(P("narrow", "wide", None), P("narrow", "wide", None), P("wide", None)),
        check_vma=False,
    )
```

time: 32.8 us -> 22.6 us (0.69)
  Pallas kernels: 25.4 us -> 19.1 us
  local copies, waits for them, and re-layouts: 6.39 us -> 2.69 us
    pallas_call x1, Pallas kernels: 25.4 us -> 19.1 us  [shards(): pl.pallas_call(functools.partial(kernel, wide, narrow, slots), out_shape=...]
    unnamed x15 -> x7, local copies, waits for them, and re-layouts: 6.39 us -> 2.69 us
where the time goes in v2:
time: 22.6 us; the launch traced here: 22.4 us
  Pallas kernels  19.1 us (85%)
  local copies, waits for them, and re-layouts  2.69 us (12%)
  between operations  0.65 us (3%)
    pallas_call x1, Pallas kernels, shards(): pl.pallas_call(functools.partial(kernel, wide, narrow, slots), out_shape=...  19.1 us
    unnamed x7, local copies, waits for them, and re-layouts  2.69 us

profile of v2, /device:TPU:0, one launch (start us, length us, event | category | flops | bytes accessed | tf_op | source)
XLA Modules:
  0.0 22.4 jit_solution(8067343412511820394)
XLA Ops:
  0.6 19.1 %graph_layer.1 = (bf16[1,128,128]{2,1,0:T(8,128)(2,1)}, bf16[1,128,128]{2,1,0:T(8,128)(2,1)}, f32[16,128]{1,0:T(8,128)}) custom-call(s32[1,8,8]{2,1,0:T(8,128)} %cols_hbm.1, s32[1,8]{1,0:T(1,128)} %counts_hbm.1, bf16[1,128,128]{2,1,0:T(8,128)(2,1)} %feat_hbm.1, bf16[128,128]{1,0:T(8,128)(2,1)} %weight_hbm.1, bf16[1024,128]{1,0:T(8,128)(2,1)} %bitcast.1, ...), custom_call_target="tpu_custom_call" | custom-call | flops 201326592 | bytes 393216 | tf_op jit(solution)/shard_map/graph_layer/pallas_call | solution.py:235
  19.7 0.0 copy-start
  19.7 1.4 %copy.12 = bf16[1,128,128]{2,1,0:T(8,128)(2,1)} copy(bf16[1,128,128]{2,1,0:T(8,128)(2,1)} %get-tuple-element.6) | data formatting | bytes 65536
  21.1 0.0 copy-done
  21.1 0.0 copy-start.1
  21.1 0.6 %copy.13 = bf16[1,128,128]{2,1,0:T(8,128)(2,1)} copy(bf16[1,128,128]{2,1,0:T(8,128)(2,1)S(1)} %copy-done) | data formatting | bytes 65536
  21.7 0.1 copy-done.1
  21.8 0.6 %copy.14 = f32[16,128]{1,0:T(8,128)} copy(f32[16,128]{1,0:T(8,128)S(1)} %copy-done.1) | data formatting | bytes 16384
Async XLA Ops:
  19.7 1.4 %copy-start = (bf16[1,128,128]{2,1,0:T(8,128)(2,1)S(1)}, bf16[1,128,128]{2,1,0:T(8,128)(2,1)}, u32[]{:S(2)}) copy-start(bf16[1,128,128]{2,1,0:T(8,128)(2,1)} %get-tuple-element.7) | copy-start | bytes 98308
  21.1 0.7 %copy-start.1 = (f32[16,128]{1,0:T(8,128)S(1)}, f32[16,128]{1,0:T(8,128)}, u32[]{:S(2)}) copy-start(f32[16,128]{1,0:T(8,128)} %get-tuple-element.8) | copy-start | bytes 24580

commit v3 on v2

--- a/solution.py
+++ b/solution.py
@@ -10,7 +10,7 @@
 MESH = pl.DeviceIdType.MESH
 F32 = jnp.float32
 BF16 = jnp.bfloat16
-VMEM_LIMIT = 60 * 1024 * 1024
+VMEM_LIMIT = 32 * 1024 * 1024
 
 
 def selection(cols_ref, counts_ref, row_block, blocks, slots, chunk):
@@ -60,6 +60,7 @@
     z, core = me // 2, lax.rem(me, 2)
     other = 1 - core
     sibling = 2 * z + other
+    across = 2 * partner(z, 1) + other
     nodes = feat_hbm.shape[1]
     tile = tiles_hbm.shape[1]
     chunk = tile // slots
@@ -75,7 +76,8 @@
     barrier = pltpu.get_barrier_semaphore()
     for k in order:
         pl.semaphore_signal(barrier, inc=1, device_id={"wide": peer(k)}, device_id_type=MESH)
-    pl.semaphore_signal(barrier, inc=1, device_id={"wide": sibling}, device_id_type=MESH)
+    for device in (sibling, across):
+        pl.semaphore_signal(barrier, inc=1, device_id={"wide": device}, device_id_type=MESH)
     for j in range(1, narrow):
         pl.semaphore_signal(barrier, inc=1, device_id={"narrow": narrow_peer(j)}, device_id_type=MESH)
 
@@ -91,13 +93,19 @@
     ]
     for load in loads:
         load.start()
-    pl.semaphore_wait(barrier, zs + narrow - 1)
+    pl.semaphore_wait(barrier, zs + narrow)
 
     def feat_copy(k, slot):
         return pltpu.make_async_remote_copy(
             src_ref=feat_hbm.at[0], dst_ref=gathered.at[rows_of(slot)],
             send_sem=f_send.at[k - 1], recv_sem=f_recv.at[k - 1],
             device_id={"wide": peer(k)}, device_id_type=MESH)
+
+    def across_copy(slot):
+        return pltpu.make_async_remote_copy(
+            src_ref=feat_hbm.at[0], dst_ref=gathered.at[rows_of(slot)],
+            send_sem=f_send.at[zs - 1], recv_sem=f_recv.at[zs - 1],
+            device_id={"wide": across}, device_id_type=MESH)
 
     def forward_copy(k, slot):
         return pltpu.make_async_remote_copy(
@@ -117,6 +125,7 @@
 
     for k in order:
         feat_copy(k, me).start()
+    across_copy(me).start()
     for copy in swap_copies(core, me):
         copy.start()
     for load in loads:
@@ -132,19 +141,28 @@
             for c in range(wide):
                 adj[rows, c * tile:(c + 1) * tile] = part[c * chunk:(c + 1) * chunk]
 
+    def mix(chip):
+        span = pl.ds(pl.multiple_of(chip * 2 * tile, 2 * tile), 2 * tile)
+        return jnp.dot(adj[:, span], gathered[span, :], preferred_element_type=F32)
+
     build(core)
     swapped = swap_copies(other, sibling)
+    feat_copy(order[0], peer(order[0])).wait_recv()
+    forward_copy(order[0], peer(order[0])).start()
     swapped[0].wait_recv()
     build(other)
-    for k in order:
+    for k in order[1:-1]:
         feat_copy(k, peer(k)).wait_recv()
         forward_copy(k, peer(k)).start()
     swapped[1].wait_recv()
     swapped[2].wait_recv()
-    for k in order:
+    mixed = mix(z)
+    feat_copy(1, peer(1)).wait_recv()
+    across_copy(across).wait_recv()
+    mixed = mixed + mix(partner(z, 1))
+    for k in order[:-1]:
         forward_copy(k, 2 * partner(z, k) + other).wait_recv()
-
-    mixed = jnp.dot(adj[...], gathered[...], preferred_element_type=F32)
+        mixed = mixed + mix(partner(z, k))
     mixed_hi = mixed.astype(BF16)
     mixed_lo = (mixed - mixed_hi.astype(F32)).astype(BF16)
     weight = weight_ref[...]
@@ -210,34 +228,46 @@
         total = total + nbuf[j]
     wgrad_ref[...] = total
 
-    for copy in swap_copies(core, me):
+    for copy in swap_copies(core, me) + [across_copy(me)]:
         copy.wait_send()
     for k in order:
         feat_copy(k, me).wait_send()
-        forward_copy(k, peer(k)).wait_send()
+        if k > 1:
+            forward_copy(k, peer(k)).wait_send()
         weight_copy(k).wait_send()
         term_copy(k).wait_send()
     for j in range(1, narrow):
         narrow_copy(j, grp).wait_send()
+
+
+def hand_over(act_ref, fgrad_ref, wgrad_ref, act_out, fgrad_out, wgrad_out, sems):
+    copies = [
+        pltpu.make_async_copy(src, dst, sems.at[i])
+        for i, (src, dst) in enumerate(((act_ref, act_out), (fgrad_ref, fgrad_out), (wgrad_ref, wgrad_out)))
+    ]
+    for copy in copies:
+        copy.start()
+    for copy in copies:
+        copy.wait()
 
 
 def shards(wide, narrow, features, weight, tiles, tile_cols, tile_counts, cotangent):
     _, nodes, width = features.shape
     slots, tile = tiles.shape[2:]
     zs = wide // 2
-    if nodes != tile or 2 * zs != wide or zs & (zs - 1):
+    if nodes != tile or 2 * zs != wide or zs < 4 or zs & (zs - 1):
         raise ValueError("mesh shape")
     share = width // wide
     vmem = pl.BlockSpec(memory_space=pltpu.VMEM)
     hbm = pl.BlockSpec(memory_space=pltpu.HBM)
     dma = pltpu.SemaphoreType.DMA
     flops = 2 * nodes * tile * width * (5 * wide + 8)
-    return pl.pallas_call(
+    results = pl.pallas_call(
         functools.partial(kernel, wide, narrow, slots),
         out_shape=(
-            jax.ShapeDtypeStruct((1, nodes, width), BF16),
-            jax.ShapeDtypeStruct((1, nodes, width), BF16),
-            jax.ShapeDtypeStruct((share, width), F32),
+            pltpu.VMEM((1, nodes, width), BF16),
+            pltpu.VMEM((1, nodes, width), BF16),
+            pltpu.VMEM((share, width), F32),
         ),
         in_specs=[hbm] * 6,
         out_specs=(vmem, vmem, vmem),
@@ -256,7 +286,7 @@
             pltpu.VMEM((zs - 1, share, width), F32),
             pltpu.VMEM((narrow, share, width), F32),
             dma((6,)),
-            dma((zs - 1,)), dma((zs - 1,)),
+            dma((zs,)), dma((zs,)),
             dma((zs - 1,)), dma((zs - 1,)),
             dma((3,)), dma((3,)),
             dma((zs - 1,)), dma((zs - 1,)),
@@ -268,7 +298,16 @@
         cost_estimate=pl.CostEstimate(
             flops=flops, bytes_accessed=2 * nodes * width * (slots + 4), transcendentals=2 * nodes * width),
         name="graph_layer",
-    )(tile_cols, tile_counts, features, weight, tiles.reshape(nodes * slots, tile), cotangent)
+    )(*(pltpu.with_memory_space_constraint(x, pltpu.HBM) for x in (
+        tile_cols, tile_counts, features, weight, tiles.reshape(nodes * slots, tile), cotangent)))
+    return pl.pallas_call(
+        hand_over,
+        out_shape=tuple(jax.ShapeDtypeStruct(r.shape, r.dtype) for r in results),
+        in_specs=[vmem] * 3,
+        out_specs=(hbm,) * 3,
+        scratch_shapes=[dma((3,))],
+        name="hand_over",
+    )(*results)
 
 
 def solution(mesh):

time: 22.6 us -> 23.1 us (1.022)
  Pallas kernels: 19.1 us -> 20.5 us
  local copies, waits for them, and re-layouts: 2.69 us -> 1.79 us
    pallas_call x0 -> x1, Pallas kernels: none -> 1.43 us  [shards(): pl.pallas_call(hand_over, out_shape=tuple((jax.ShapeDtypeStruct(r.shape,...]
    unnamed x7 -> x6, local copies, waits for them, and re-layouts: 2.69 us -> 1.79 us
where the time goes in v3:
time: 23.1 us; the launch traced here: 22.9 us
  Pallas kernels  20.5 us (89%)
  local copies, waits for them, and re-layouts  1.79 us (8%)
  between operations  0.65 us (3%)
    pallas_call x1, Pallas kernels, shards(): pl.pallas_call(functools.partial(kernel, wide, narrow, slots), out_shape=...  19 us
    unnamed x6, local copies, waits for them, and re-layouts  1.79 us
    pallas_call x1, Pallas kernels, shards(): pl.pallas_call(hand_over, out_shape=tuple((jax.ShapeDtypeStruct(r.shape,...  1.43 us

profile of v3, /device:TPU:0, one launch (start us, length us, event | category | flops | bytes accessed | tf_op | source)
XLA Modules:
  0.0 22.9 jit_solution(8464510660109414570)
XLA Ops:
  0.6 19.0 %graph_layer.1 = (bf16[1,128,128]{2,1,0:T(8,128)(2,1)S(1)}, bf16[1,128,128]{2,1,0:T(8,128)(2,1)S(1)}, f32[16,128]{1,0:T(8,128)S(1)}) custom-call(s32[1,8,8]{2,1,0:T(8,128)} %cols_hbm.1, s32[1,8]{1,0:T(1,128)} %counts_hbm.1, bf16[1,128,128]{2,1,0:T(8,128)(2,1)} %feat_hbm.1, bf16[128,128]{1,0:T(8,128)(2,1)} %weight_hbm.1, bf16[1024,128]{1,0:T(8,128)(2,1)} %bitcast.1, ...), custom_call_target="tpu_custom_call" | custom-call | flops 201326592 | bytes 393216 | tf_op jit(solution)/shard_map/graph_layer/pallas_call | solution.py:265
  19.7 0.0 copy-start
  19.7 0.6 %copy-done = bf16[1,128,128]{2,1,0:T(8,128)(2,1)} copy-done((bf16[1,128,128]{2,1,0:T(8,128)(2,1)}, bf16[1,128,128]{2,1,0:T(8,128)(2,1)S(1)}, u32[]{:S(2)}) %copy-start) | copy-done | bytes 32792
  20.3 0.0 copy-start.1
  20.3 0.6 %copy-done.1 = bf16[1,128,128]{2,1,0:T(8,128)(2,1)} copy-done((bf16[1,128,128]{2,1,0:T(8,128)(2,1)}, bf16[1,128,128]{2,1,0:T(8,128)(2,1)S(1)}, u32[]{:S(2)}) %copy-start.1) | copy-done | bytes 32792
  20.9 0.0 copy-start.2
  20.9 0.6 %copy-done.2 = f32[16,128]{1,0:T(8,128)} copy-done((f32[16,128]{1,0:T(8,128)}, f32[16,128]{1,0:T(8,128)S(1)}, u32[]{:S(2)}) %copy-start.2) | copy-done | bytes 8216
  21.5 1.4 %hand_over.1 = (bf16[1,128,128]{2,1,0:T(8,128)(2,1)}, bf16[1,128,128]{2,1,0:T(8,128)(2,1)}, f32[16,128]{1,0:T(8,128)}) custom-call(bf16[1,128,128]{2,1,0:T(8,128)(2,1)} %copy-done, bf16[1,128,128]{2,1,0:T(8,128)(2,1)} %copy-done.1, f32[16,128]{1,0:T(8,128)} %copy-done.2), custom_call_target="tpu_custom_call" | custom-call | tf_op jit(solution)/shard_map/hand_over/pallas_call | solution.py:303
Async XLA Ops:
  19.7 0.6 %copy-start = (bf16[1,128,128]{2,1,0:T(8,128)(2,1)}, bf16[1,128,128]{2,1,0:T(8,128)(2,1)S(1)}, u32[]{:S(2)}) copy-start(bf16[1,128,128]{2,1,0:T(8,128)(2,1)S(1)} %get-tuple-element.6.act_ref) | copy-start | bytes 98308
  20.3 0.6 %copy-start.1 = (bf16[1,128,128]{2,1,0:T(8,128)(2,1)}, bf16[1,128,128]{2,1,0:T(8,128)(2,1)S(1)}, u32[]{:S(2)}) copy-start(bf16[1,128,128]{2,1,0:T(8,128)(2,1)S(1)} %get-tuple-element.7.fgrad_ref) | copy-start | bytes 98308
  20.9 0.6 %copy-start.2 = (f32[16,128]{1,0:T(8,128)}, f32[16,128]{1,0:T(8,128)S(1)}, u32[]{:S(2)}) copy-start(f32[16,128]{1,0:T(8,128)S(1)} %get-tuple-element.8.wgrad_ref) | copy-start | bytes 24580

commit v4 on v3

--- a/solution.py
+++ b/solution.py
@@ -166,8 +166,9 @@
     mixed_hi = mixed.astype(BF16)
     mixed_lo = (mixed - mixed_hi.astype(F32)).astype(BF16)
     weight = weight_ref[...]
-    pre_act = (jnp.dot(mixed_hi, weight, preferred_element_type=F32)
-               + jnp.dot(mixed_lo, weight, preferred_element_type=F32))
+    pre_act = jnp.dot(
+        jnp.concatenate([mixed_hi, mixed_lo], axis=1), jnp.concatenate([weight, weight], axis=0),
+        preferred_element_type=F32)
     sig_val = jax.nn.sigmoid(pre_act)
     acts[...] = (pre_act * sig_val).astype(BF16).reshape(acts.shape)
     cot = cot_ref[...].reshape(2 * nodes, -1).astype(F32)
@@ -306,8 +307,9 @@
         in_specs=[vmem] * 3,
         out_specs=(hbm,) * 3,
         scratch_shapes=[dma((3,))],
+        compiler_params=pltpu.CompilerParams(vmem_limit_bytes=2 * 1024 * 1024),
         name="hand_over",
-    )(*results)
+    )(*(pltpu.with_memory_space_constraint(r, pltpu.VMEM) for r in results))
 
 
 def solution(mesh):

time: 23.1 us -> 20.5 us (0.89)
  local copies, waits for them, and re-layouts: 1.79 us -> 0 us
  Pallas kernels: 20.5 us -> 19.7 us
    unnamed x6 -> x0, local copies, waits for them, and re-layouts: 1.79 us -> none
    pallas_call x1, Pallas kernels: 1.43 us -> 0.66 us  [shards(): pl.pallas_call(hand_over, out_shape=tuple((jax.ShapeDtypeStruct(r.shape,...]
where the time goes in v4:
time: 20.5 us; the launch traced here: 20.3 us
  Pallas kernels  19.7 us (96%)
  between operations  0.64 us (3%)
    pallas_call x1, Pallas kernels, shards(): pl.pallas_call(functools.partial(kernel, wide, narrow, slots), out_shape=...  19 us
    pallas_call x1, Pallas kernels, shards(): pl.pallas_call(hand_over, out_shape=tuple((jax.ShapeDtypeStruct(r.shape,...  0.66 us

profile of v4, /device:TPU:0, one launch (start us, length us, event | category | flops | bytes accessed | tf_op | source)
XLA Modules:
  0.0 20.3 jit_solution(17008053993205626914)
XLA Ops:
  0.6 19.0 %graph_layer.1 = (bf16[1,128,128]{2,1,0:T(8,128)(2,1)S(1)}, bf16[1,128,128]{2,1,0:T(8,128)(2,1)S(1)}, f32[16,128]{1,0:T(8,128)S(1)}) custom-call(s32[1,8,8]{2,1,0:T(8,128)} %cols_hbm.1, s32[1,8]{1,0:T(1,128)} %counts_hbm.1, bf16[1,128,128]{2,1,0:T(8,128)(2,1)} %feat_hbm.1, bf16[128,128]{1,0:T(8,128)(2,1)} %weight_hbm.1, bf16[1024,128]{1,0:T(8,128)(2,1)} %bitcast.1, ...), custom_call_target="tpu_custom_call" | custom-call | flops 201326592 | bytes 393216 | tf_op jit(solution)/shard_map/graph_layer/pallas_call | solution.py:266
  19.7 0.7 %hand_over.1 = (bf16[1,128,128]{2,1,0:T(8,128)(2,1)}, bf16[1,128,128]{2,1,0:T(8,128)(2,1)}, f32[16,128]{1,0:T(8,128)}) custom-call(bf16[1,128,128]{2,1,0:T(8,128)(2,1)S(1)} %get-tuple-element.6.act_ref, bf16[1,128,128]{2,1,0:T(8,128)(2,1)S(1)} %get-tuple-element.7.fgrad_ref, f32[16,128]{1,0:T(8,128)S(1)} %get-tuple-element.8.wgrad_ref), custom_call_target="tpu_custom_call" | custom-call | tf_op jit(solution)/shard_map/hand_over/pallas_call | solution.py:304

commit v5 on v4

--- a/solution.py
+++ b/solution.py
@@ -91,8 +91,6 @@
             (feat_hbm.at[0], gathered.at[rows_of(me)]), (weight_hbm, weight_ref),
             (cot_hbm.at[0], cot_ref.at[core])))
     ]
-    for load in loads:
-        load.start()
     pl.semaphore_wait(barrier, zs + narrow)
 
     def feat_copy(k, slot):
@@ -128,6 +126,8 @@
     across_copy(me).start()
     for copy in swap_copies(core, me):
         copy.start()
+    for load in loads:
+        load.start()
     for load in loads:
         load.wait()
 
@@ -180,6 +180,19 @@
             send_sem=w_send.at[k - 1], recv_sem=w_recv.at[k - 1],
             device_id={"wide": peer(k)}, device_id_type=MESH)
 
+    back = lax.dot_general(weight, act_grad, (((1,), (1,)), ((), ())), preferred_element_type=F32).astype(BF16)
+
+    def term_copy(k):
+        return pltpu.make_async_remote_copy(
+            src_ref=terms.at[k - 1], dst_ref=incoming.at[k - 1],
+            send_sem=t_send.at[k - 1], recv_sem=t_recv.at[k - 1],
+            device_id={"wide": peer(k)}, device_id_type=MESH)
+
+    def send_term(k):
+        terms[k - 1] = jnp.dot(back, adj[:, rows_of(peer(k))], preferred_element_type=F32).astype(BF16)
+        term_copy(k).start()
+
+    send_term(order[0])
     weight_part = lax.dot_general(
         mixed_hi, act_grad, (((0,), (0,)), ((), ())), preferred_element_type=F32)
     for c in range(wide):
@@ -187,17 +200,8 @@
     for k in order:
         weight_copy(k).start()
 
-    back = lax.dot_general(weight, act_grad, (((1,), (1,)), ((), ())), preferred_element_type=F32).astype(BF16)
-
-    def term_copy(k):
-        return pltpu.make_async_remote_copy(
-            src_ref=terms.at[k - 1], dst_ref=incoming.at[k - 1],
-            send_sem=t_send.at[k - 1], recv_sem=t_recv.at[k - 1],
-            device_id={"wide": peer(k)}, device_id_type=MESH)
-
-    for k in order:
-        terms[k - 1] = jnp.dot(back, adj[:, rows_of(peer(k))], preferred_element_type=F32).astype(BF16)
-        term_copy(k).start()
+    for k in order[1:]:
+        send_term(k)
 
     own = jnp.dot(back, adj[:, rows_of(me)], preferred_element_type=F32)
     act_ref[0] = acts[core]

time: 20.5 us -> 21.3 us (1.039)
  Pallas kernels: 19.7 us -> 20.5 us
    pallas_call x1, Pallas kernels: 19 us -> 19.8 us  [shards(): pl.pallas_call(functools.partial(kernel, wide, narrow, slots), out_shape=...]
where the time goes in v5:
time: 21.3 us; the launch traced here: 21.1 us
  Pallas kernels  20.5 us (96%)
  between operations  0.64 us (3%)
    pallas_call x1, Pallas kernels, shards(): pl.pallas_call(functools.partial(kernel, wide, narrow, slots), out_shape=...  19.8 us
    pallas_call x1, Pallas kernels, shards(): pl.pallas_call(hand_over, out_shape=tuple((jax.ShapeDtypeStruct(r.shape,...  0.66 us

profile of v5, /device:TPU:0, one launch (start us, length us, event | category | flops | bytes accessed | tf_op | source)
XLA Modules:
  0.0 21.1 jit_solution(2922246558688352110)
XLA Ops:
  0.6 19.8 %graph_layer.1 = (bf16[1,128,128]{2,1,0:T(8,128)(2,1)S(1)}, bf16[1,128,128]{2,1,0:T(8,128)(2,1)S(1)}, f32[16,128]{1,0:T(8,128)S(1)}) custom-call(s32[1,8,8]{2,1,0:T(8,128)} %cols_hbm.1, s32[1,8]{1,0:T(1,128)} %counts_hbm.1, bf16[1,128,128]{2,1,0:T(8,128)(2,1)} %feat_hbm.1, bf16[128,128]{1,0:T(8,128)(2,1)} %weight_hbm.1, bf16[1024,128]{1,0:T(8,128)(2,1)} %bitcast.1, ...), custom_call_target="tpu_custom_call" | custom-call | flops 201326592 | bytes 393216 | tf_op jit(solution)/shard_map/graph_layer/pallas_call | solution.py:270
  20.5 0.7 %hand_over.1 = (bf16[1,128,128]{2,1,0:T(8,128)(2,1)}, bf16[1,128,128]{2,1,0:T(8,128)(2,1)}, f32[16,128]{1,0:T(8,128)}) custom-call(bf16[1,128,128]{2,1,0:T(8,128)(2,1)S(1)} %get-tuple-element.6.act_ref, bf16[1,128,128]{2,1,0:T(8,128)(2,1)S(1)} %get-tuple-element.7.fgrad_ref, f32[16,128]{1,0:T(8,128)S(1)} %get-tuple-element.8.wgrad_ref), custom_call_target="tpu_custom_call" | custom-call | tf_op jit(solution)/shard_map/hand_over/pallas_call | solution.py:308

commit v6 on v4

--- a/solution.py
+++ b/solution.py
@@ -114,8 +114,9 @@
             device_id={"wide": sibling}, device_id_type=MESH)
 
     def swap_copies(half, slot):
-        pairs = ((tiles_hbm, tiles_ref.at[half]), (feat_hbm.at[0], gathered.at[rows_of(slot)]),
-                 (cot_hbm.at[0], cot_ref.at[half]))
+        piece = nodes * slots // 2
+        pairs = [(tiles_hbm.at[pl.ds(i * piece, piece)], tiles_ref.at[half, pl.ds(i * piece, piece)]) for i in range(2)]
+        pairs += [(feat_hbm.at[0], gathered.at[rows_of(slot)]), (cot_hbm.at[0], cot_ref.at[half])]
         return [
             pltpu.make_async_remote_copy(
                 src_ref=src, dst_ref=dst, send_sem=s_send.at[i], recv_sem=s_recv.at[i],
@@ -123,39 +124,51 @@
             for i, (src, dst) in enumerate(pairs)
         ]
 
-    for k in order:
+    outgoing = swap_copies(core, me)
+    for k in order[:-1]:
         feat_copy(k, me).start()
+    outgoing[0].start()
+    outgoing[1].start()
+    feat_copy(1, me).start()
     across_copy(me).start()
-    for copy in swap_copies(core, me):
-        copy.start()
-    for load in loads:
+    outgoing[2].start()
+    outgoing[3].start()
+    for load in loads[:3]:
         load.wait()
 
-    def build(half):
-        pick = selection(cols_ref, counts_ref, 2 * z + half, wide, slots, chunk)
-        base = half * nodes
-        for j in range(nodes // chunk):
-            part = jnp.dot(
-                pick, tiles_ref[half, j * tile:(j + 1) * tile, :], preferred_element_type=F32).astype(BF16)
-            rows = pl.ds(pl.multiple_of(base + j * chunk, chunk), chunk)
-            for c in range(wide):
-                adj[rows, c * tile:(c + 1) * tile] = part[c * chunk:(c + 1) * chunk]
+    def build(half, pick, piece):
+        count = nodes // chunk // 2
+        for j in range(piece * count, (piece + 1) * count, 2):
+            both = jnp.concatenate(
+                [tiles_ref[half, i * tile:(i + 1) * tile, :] for i in (j, j + 1)], axis=1)
+            part = jnp.dot(pick, both, preferred_element_type=F32).astype(BF16)
+            for i in range(2):
+                rows = pl.ds(pl.multiple_of(half * nodes + (j + i) * chunk, chunk), chunk)
+                for c in range(wide):
+                    adj[rows, c * tile:(c + 1) * tile] = part[
+                        c * chunk:(c + 1) * chunk, i * tile:(i + 1) * tile]
 
     def mix(chip):
         span = pl.ds(pl.multiple_of(chip * 2 * tile, 2 * tile), 2 * tile)
         return jnp.dot(adj[:, span], gathered[span, :], preferred_element_type=F32)
 
-    build(core)
+    pick = selection(cols_ref, counts_ref, 2 * z + core, wide, slots, chunk)
+    build(core, pick, 0)
+    build(core, pick, 1)
+    pick = selection(cols_ref, counts_ref, 2 * z + other, wide, slots, chunk)
     swapped = swap_copies(other, sibling)
     feat_copy(order[0], peer(order[0])).wait_recv()
     forward_copy(order[0], peer(order[0])).start()
-    swapped[0].wait_recv()
-    build(other)
+    for piece in range(2):
+        swapped[piece].wait_recv()
+        build(other, pick, piece)
     for k in order[1:-1]:
         feat_copy(k, peer(k)).wait_recv()
         forward_copy(k, peer(k)).start()
-    swapped[1].wait_recv()
+    for load in loads[3:]:
+        load.wait()
     swapped[2].wait_recv()
+    swapped[3].wait_recv()
     mixed = mix(z)
     feat_copy(1, peer(1)).wait_recv()
     across_copy(across).wait_recv()
@@ -289,7 +302,7 @@
             dma((6,)),
             dma((zs,)), dma((zs,)),
             dma((zs - 1,)), dma((zs - 1,)),
-            dma((3,)), dma((3,)),
+            dma((4,)), dma((4,)),
             dma((zs - 1,)), dma((zs - 1,)),
             dma((zs - 1,)), dma((zs - 1,)),
             dma((narrow - 1,)), dma((narrow - 1,)),

time: 20.5 us -> 20.5 us (level)
  no operation moved by 1% of the time
where the time goes in v6:
time: 20.5 us; the launch traced here: 20.3 us
  Pallas kernels  19.7 us (96%)
  between operations  0.64 us (3%)
    pallas_call x1, Pallas kernels, shards(): pl.pallas_call(functools.partial(kernel, wide, narrow, slots), out_shape=...  19 us
    pallas_call x1, Pallas kernels, shards(): pl.pallas_call(hand_over, out_shape=tuple((jax.ShapeDtypeStruct(r.shape,...  0.66 us

profile of v6, /device:TPU:0, one launch (start us, length us, event | category | flops | bytes accessed | tf_op | source)
XLA Modules:
  0.0 20.3 jit_solution(8588097776997964159)
XLA Ops:
  0.6 19.0 %graph_layer.1 = (bf16[1,128,128]{2,1,0:T(8,128)(2,1)S(1)}, bf16[1,128,128]{2,1,0:T(8,128)(2,1)S(1)}, f32[16,128]{1,0:T(8,128)S(1)}) custom-call(s32[1,8,8]{2,1,0:T(8,128)} %cols_hbm.1, s32[1,8]{1,0:T(1,128)} %counts_hbm.1, bf16[1,128,128]{2,1,0:T(8,128)(2,1)} %feat_hbm.1, bf16[128,128]{1,0:T(8,128)(2,1)} %weight_hbm.1, bf16[1024,128]{1,0:T(8,128)(2,1)} %bitcast.1, ...), custom_call_target="tpu_custom_call" | custom-call | flops 201326592 | bytes 393216 | tf_op jit(solution)/shard_map/graph_layer/pallas_call | solution.py:279
  19.7 0.7 %hand_over.1 = (bf16[1,128,128]{2,1,0:T(8,128)(2,1)}, bf16[1,128,128]{2,1,0:T(8,128)(2,1)}, f32[16,128]{1,0:T(8,128)}) custom-call(bf16[1,128,128]{2,1,0:T(8,128)(2,1)S(1)} %get-tuple-element.6.act_ref, bf16[1,128,128]{2,1,0:T(8,128)(2,1)S(1)} %get-tuple-element.7.fgrad_ref, f32[16,128]{1,0:T(8,128)S(1)} %get-tuple-element.8.wgrad_ref), custom_call_target="tpu_custom_call" | custom-call | tf_op jit(solution)/shard_map/hand_over/pallas_call | solution.py:317

commit v7 on v6

--- a/solution.py
+++ b/solution.py
@@ -208,12 +208,12 @@
             send_sem=t_send.at[k - 1], recv_sem=t_recv.at[k - 1],
             device_id={"wide": peer(k)}, device_id_type=MESH)
 
-    for k in order:
+    def send_term(k):
         terms[k - 1] = jnp.dot(back, adj[:, rows_of(peer(k))], preferred_element_type=F32).astype(BF16)
         term_copy(k).start()
 
-    own = jnp.dot(back, adj[:, rows_of(me)], preferred_element_type=F32)
-    act_ref[0] = acts[core]
+    for k in order[:-1]:
+        send_term(k)
 
     wsum = wpart[me]
     for k in order:
@@ -229,6 +229,10 @@
 
     for j in range(1, narrow):
         narrow_copy(j, grp).start()
+
+    send_term(1)
+    own = jnp.dot(back, adj[:, rows_of(me)], preferred_element_type=F32)
+    act_ref[0] = acts[core]
 
     for k in order:
         term_copy(k).wait_recv()

time: 20.5 us -> 20.5 us (level)
  no operation moved by 1% of the time
where the time goes in v7:
time: 20.5 us; the launch traced here: 20.3 us
  Pallas kernels  19.7 us (96%)
  between operations  0.64 us (3%)
    pallas_call x1, Pallas kernels, shards(): pl.pallas_call(functools.partial(kernel, wide, narrow, slots), out_shape=...  19 us
    pallas_call x1, Pallas kernels, shards(): pl.pallas_call(hand_over, out_shape=tuple((jax.ShapeDtypeStruct(r.shape,...  0.66 us

profile of v7, /device:TPU:0, one launch (start us, length us, event | category | flops | bytes accessed | tf_op | source)
XLA Modules:
  0.0 20.3 jit_solution(16692088102367810296)
XLA Ops:
  0.6 19.0 %graph_layer.1 = (bf16[1,128,128]{2,1,0:T(8,128)(2,1)S(1)}, bf16[1,128,128]{2,1,0:T(8,128)(2,1)S(1)}, f32[16,128]{1,0:T(8,128)S(1)}) custom-call(s32[1,8,8]{2,1,0:T(8,128)} %cols_hbm.1, s32[1,8]{1,0:T(1,128)} %counts_hbm.1, bf16[1,128,128]{2,1,0:T(8,128)(2,1)} %feat_hbm.1, bf16[128,128]{1,0:T(8,128)(2,1)} %weight_hbm.1, bf16[1024,128]{1,0:T(8,128)(2,1)} %bitcast.1, ...), custom_call_target="tpu_custom_call" | custom-call | flops 201326592 | bytes 393216 | tf_op jit(solution)/shard_map/graph_layer/pallas_call | solution.py:283
  19.7 0.7 %hand_over.1 = (bf16[1,128,128]{2,1,0:T(8,128)(2,1)}, bf16[1,128,128]{2,1,0:T(8,128)(2,1)}, f32[16,128]{1,0:T(8,128)}) custom-call(bf16[1,128,128]{2,1,0:T(8,128)(2,1)S(1)} %get-tuple-element.6.act_ref, bf16[1,128,128]{2,1,0:T(8,128)(2,1)S(1)} %get-tuple-element.7.fgrad_ref, f32[16,128]{1,0:T(8,128)S(1)} %get-tuple-element.8.wgrad_ref), custom_call_target="tpu_custom_call" | custom-call | tf_op jit(solution)/shard_map/hand_over/pallas_call | solution.py:321

commit v8 on v7

--- a/solution.py
+++ b/solution.py
@@ -87,23 +87,24 @@
     loads = [
         pltpu.make_async_copy(src, dst, in_sems.at[i])
         for i, (src, dst) in enumerate((
-            (cols_hbm, cols_ref), (counts_hbm, counts_ref), (tiles_hbm, tiles_ref.at[core]),
-            (feat_hbm.at[0], gathered.at[rows_of(me)]), (weight_hbm, weight_ref),
+            (feat_hbm.at[0], gathered.at[rows_of(me)]),
+            (cols_hbm, cols_ref), (counts_hbm, counts_ref), (tiles_hbm, tiles_ref.at[core]), (weight_hbm, weight_ref),
             (cot_hbm.at[0], cot_ref.at[core])))
     ]
     for load in loads:
         load.start()
+    loads[0].wait()
     pl.semaphore_wait(barrier, zs + narrow)
 
     def feat_copy(k, slot):
         return pltpu.make_async_remote_copy(
-            src_ref=feat_hbm.at[0], dst_ref=gathered.at[rows_of(slot)],
+            src_ref=gathered.at[rows_of(me)], dst_ref=gathered.at[rows_of(slot)],
             send_sem=f_send.at[k - 1], recv_sem=f_recv.at[k - 1],
             device_id={"wide": peer(k)}, device_id_type=MESH)
 
     def across_copy(slot):
         return pltpu.make_async_remote_copy(
-            src_ref=feat_hbm.at[0], dst_ref=gathered.at[rows_of(slot)],
+            src_ref=gathered.at[rows_of(me)], dst_ref=gathered.at[rows_of(slot)],
             send_sem=f_send.at[zs - 1], recv_sem=f_recv.at[zs - 1],
             device_id={"wide": across}, device_id_type=MESH)
 
@@ -116,7 +117,7 @@
     def swap_copies(half, slot):
         piece = nodes * slots // 2
         pairs = [(tiles_hbm.at[pl.ds(i * piece, piece)], tiles_ref.at[half, pl.ds(i * piece, piece)]) for i in range(2)]
-        pairs += [(feat_hbm.at[0], gathered.at[rows_of(slot)]), (cot_hbm.at[0], cot_ref.at[half])]
+        pairs += [(gathered.at[rows_of(slot)], gathered.at[rows_of(slot)]), (cot_hbm.at[0], cot_ref.at[half])]
         return [
             pltpu.make_async_remote_copy(
                 src_ref=src, dst_ref=dst, send_sem=s_send.at[i], recv_sem=s_recv.at[i],
@@ -133,7 +134,7 @@
     across_copy(me).start()
     outgoing[2].start()
     outgoing[3].start()
-    for load in loads[:3]:
+    for load in loads[1:4]:
         load.wait()
 
     def build(half, pick, piece):
@@ -165,7 +166,7 @@
     for k in order[1:-1]:
         feat_copy(k, peer(k)).wait_recv()
         forward_copy(k, peer(k)).start()
-    for load in loads[3:]:
+    for load in loads[4:]:
         load.wait()
     swapped[2].wait_recv()
     swapped[3].wait_recv()
@@ -193,6 +194,19 @@
             send_sem=w_send.at[k - 1], recv_sem=w_recv.at[k - 1],
             device_id={"wide": peer(k)}, device_id_type=MESH)
 
+    back = lax.dot_general(weight, act_grad, (((1,), (1,)), ((), ())), preferred_element_type=F32).astype(BF16)
+
+    def term_copy(k):
+        return pltpu.make_async_remote_copy(
+            src_ref=terms.at[k - 1], dst_ref=incoming.at[k - 1],
+            send_sem=t_send.at[k - 1], recv_sem=t_recv.at[k - 1],
+            device_id={"wide": peer(k)}, device_id_type=MESH)
+
+    def send_term(k):
+        terms[k - 1] = jnp.dot(back, adj[:, rows_of(peer(k))], preferred_element_type=F32).astype(BF16)
+        term_copy(k).start()
+
+    send_term(order[0])
     weight_part = lax.dot_general(
         mixed_hi, act_grad, (((0,), (0,)), ((), ())), preferred_element_type=F32)
     for c in range(wide):
@@ -200,19 +214,7 @@
     for k in order:
         weight_copy(k).start()
 
-    back = lax.dot_general(weight, act_grad, (((1,), (1,)), ((), ())), preferred_element_type=F32).astype(BF16)
-
-    def term_copy(k):
-        return pltpu.make_async_remote_copy(
-            src_ref=terms.at[k - 1], dst_ref=incoming.at[k - 1],
-            send_sem=t_send.at[k - 1], recv_sem=t_recv.at[k - 1],
-            device_id={"wide": peer(k)}, device_id_type=MESH)
-
-    def send_term(k):
-        terms[k - 1] = jnp.dot(back, adj[:, rows_of(peer(k))], preferred_element_type=F32).astype(BF16)
-        term_copy(k).start()
-
-    for k in order[:-1]:
+    for k in order[1:-1]:
         send_term(k)
 
     wsum = wpart[me]

time: 20.5 us -> 21.1 us (1.029)
  Pallas kernels: 19.7 us -> 20.3 us
    pallas_call x1, Pallas kernels: 19 us -> 19.7 us  [shards(): pl.pallas_call(functools.partial(kernel, wide, narrow, slots), out_shape=...]
where the time goes in v8:
time: 21.1 us; the launch traced here: 21 us
  Pallas kernels  20.3 us (96%)
  between operations  0.64 us (3%)
    pallas_call x1, Pallas kernels, shards(): pl.pallas_call(functools.partial(kernel, wide, narrow, slots), out_shape=...  19.7 us
    pallas_call x1, Pallas kernels, shards(): pl.pallas_call(hand_over, out_shape=tuple((jax.ShapeDtypeStruct(r.shape,...  0.66 us

profile of v8, /device:TPU:0, one launch (start us, length us, event | category | flops | bytes accessed | tf_op | source)
XLA Modules:
  0.0 21.0 jit_solution(2701129690598222825)
XLA Ops:
  0.6 19.7 %graph_layer.1 = (bf16[1,128,128]{2,1,0:T(8,128)(2,1)S(1)}, bf16[1,128,128]{2,1,0:T(8,128)(2,1)S(1)}, f32[16,128]{1,0:T(8,128)S(1)}) custom-call(s32[1,8,8]{2,1,0:T(8,128)} %cols_hbm.1, s32[1,8]{1,0:T(1,128)} %counts_hbm.1, bf16[1,128,128]{2,1,0:T(8,128)(2,1)} %feat_hbm.1, bf16[128,128]{1,0:T(8,128)(2,1)} %weight_hbm.1, bf16[1024,128]{1,0:T(8,128)(2,1)} %bitcast.1, ...), custom_call_target="tpu_custom_call" | custom-call | flops 201326592 | bytes 393216 | tf_op jit(solution)/shard_map/graph_layer/pallas_call | solution.py:285
  20.3 0.7 %hand_over.1 = (bf16[1,128,128]{2,1,0:T(8,128)(2,1)}, bf16[1,128,128]{2,1,0:T(8,128)(2,1)}, f32[16,128]{1,0:T(8,128)}) custom-call(bf16[1,128,128]{2,1,0:T(8,128)(2,1)S(1)} %get-tuple-element.6.act_ref, bf16[1,128,128]{2,1,0:T(8,128)(2,1)S(1)} %get-tuple-element.7.fgrad_ref, f32[16,128]{1,0:T(8,128)S(1)} %get-tuple-element.8.wgrad_ref), custom_call_target="tpu_custom_call" | custom-call | tf_op jit(solution)/shard_map/hand_over/pallas_call | solution.py:323

commit v9 on v8

--- a/solution.py
+++ b/solution.py
@@ -194,19 +194,6 @@
             send_sem=w_send.at[k - 1], recv_sem=w_recv.at[k - 1],
             device_id={"wide": peer(k)}, device_id_type=MESH)
 
-    back = lax.dot_general(weight, act_grad, (((1,), (1,)), ((), ())), preferred_element_type=F32).astype(BF16)
-
-    def term_copy(k):
-        return pltpu.make_async_remote_copy(
-            src_ref=terms.at[k - 1], dst_ref=incoming.at[k - 1],
-            send_sem=t_send.at[k - 1], recv_sem=t_recv.at[k - 1],
-            device_id={"wide": peer(k)}, device_id_type=MESH)
-
-    def send_term(k):
-        terms[k - 1] = jnp.dot(back, adj[:, rows_of(peer(k))], preferred_element_type=F32).astype(BF16)
-        term_copy(k).start()
-
-    send_term(order[0])
     weight_part = lax.dot_general(
         mixed_hi, act_grad, (((0,), (0,)), ((), ())), preferred_element_type=F32)
     for c in range(wide):
@@ -214,7 +201,19 @@
     for k in order:
         weight_copy(k).start()
 
-    for k in order[1:-1]:
+    back = lax.dot_general(weight, act_grad, (((1,), (1,)), ((), ())), preferred_element_type=F32).astype(BF16)
+
+    def term_copy(k):
+        return pltpu.make_async_remote_copy(
+            src_ref=terms.at[k - 1], dst_ref=incoming.at[k - 1],
+            send_sem=t_send.at[k - 1], recv_sem=t_recv.at[k - 1],
+            device_id={"wide": peer(k)}, device_id_type=MESH)
+
+    def send_term(k):
+        terms[k - 1] = jnp.dot(back, adj[:, rows_of(peer(k))], preferred_element_type=F32).astype(BF16)
+        term_copy(k).start()
+
+    for k in order[:-1]:
         send_term(k)
 
     wsum = wpart[me]

time: 21.1 us -> 20.3 us (0.962)
  Pallas kernels: 20.3 us -> 19.5 us
    pallas_call x1, Pallas kernels: 19.7 us -> 18.8 us  [shards(): pl.pallas_call(functools.partial(kernel, wide, narrow, slots), out_shape=...]
where the time goes in v9:
time: 20.3 us; the launch traced here: 20.1 us
  Pallas kernels  19.5 us (96%)
  between operations  0.64 us (3%)
    pallas_call x1, Pallas kernels, shards(): pl.pallas_call(functools.partial(kernel, wide, narrow, slots), out_shape=...  18.8 us
    pallas_call x1, Pallas kernels, shards(): pl.pallas_call(hand_over, out_shape=tuple((jax.ShapeDtypeStruct(r.shape,...  0.66 us

profile of v9, /device:TPU:0, one launch (start us, length us, event | category | flops | bytes accessed | tf_op | source)
XLA Modules:
  0.0 20.1 jit_solution(10155521462135786332)
XLA Ops:
  0.6 18.8 %graph_layer.1 = (bf16[1,128,128]{2,1,0:T(8,128)(2,1)S(1)}, bf16[1,128,128]{2,1,0:T(8,128)(2,1)S(1)}, f32[16,128]{1,0:T(8,128)S(1)}) custom-call(s32[1,8,8]{2,1,0:T(8,128)} %cols_hbm.1, s32[1,8]{1,0:T(1,128)} %counts_hbm.1, bf16[1,128,128]{2,1,0:T(8,128)(2,1)} %feat_hbm.1, bf16[128,128]{1,0:T(8,128)(2,1)} %weight_hbm.1, bf16[1024,128]{1,0:T(8,128)(2,1)} %bitcast.1, ...), custom_call_target="tpu_custom_call" | custom-call | flops 201326592 | bytes 393216 | tf_op jit(solution)/shard_map/graph_layer/pallas_call | solution.py:284
  19.5 0.7 %hand_over.1 = (bf16[1,128,128]{2,1,0:T(8,128)(2,1)}, bf16[1,128,128]{2,1,0:T(8,128)(2,1)}, f32[16,128]{1,0:T(8,128)}) custom-call(bf16[1,128,128]{2,1,0:T(8,128)(2,1)S(1)} %get-tuple-element.6.act_ref, bf16[1,128,128]{2,1,0:T(8,128)(2,1)S(1)} %get-tuple-element.7.fgrad_ref, f32[16,128]{1,0:T(8,128)S(1)} %get-tuple-element.8.wgrad_ref), custom_call_target="tpu_custom_call" | custom-call | tf_op jit(solution)/shard_map/hand_over/pallas_call | solution.py:322
